TPU v7x, 128 devices: a whole 4x4x4 slice. The times are simulated.
128 devices in a mesh: batch: 8 (over z, core), table: 16 (over y, x).
Axes of the slice: x: 4, y: 4, z: 4, core: 2. Of those that a mesh axis runs over, the one named last changes fastest.
Arguments:
- item_rows: int32 [1024, 64, 3], P(('batch', 'table')), may hold values from 0 to 16383, as said below
- send_order: int32 [1024], P(('batch', 'table')), may hold values from 0 to 7, as said below
- user_lengths: int32 [1024], P(('batch', 'table')), may hold values from 1 to 64, as said below
- tables: bfloat16 [3, 16384, 1024], P(None, 'table'), may hold values from -3 to 3
- w_in: bfloat16 [1, 1024, 4096], replicated, may hold values from -0.1875 to 0.1875
- w_out: bfloat16 [1, 1024, 1024], replicated, may hold values from -0.1875 to 0.1875
- out_grad: bfloat16 [1024, 64, 1024], P(('batch', 'table')), may hold values from -6 to 6
Outputs:
- encoded: bfloat16 [1024, 64, 1024], P(('batch', 'table'))
- table_grad: float32 [3, 16384, 1024], P(None, 'table', 'batch')
Inputs may be any that keep to these rules, and one draw needn't show every extreme that they name: `item_rows`: every id lies in one table's rows. For each user, the 192 ids name rows of each block of 1024 rows exactly 12 times; padded slots carry ids too. `send_order`: each block of 8 entries is a permutation of 0 to 7. `user_lengths`: the first user of every block of 8 has length 64.
All inputs are finite; a program needn't handle non-finite values.
Results may differ from a plain program's by a relative error of at most 0.013.
Values may be sent and summed in bfloat16 or wider, within the bound.
No kernel may reach another device: no remote copies, remote signals or barrier semaphores. Data moves between devices by JAX's collectives and lax.ppermute only.
A program may use at most 192 MiB of HBM per device.

v0:
```python
import functools

import jax
import jax.numpy as jnp
from jax import lax
from jax.experimental import pallas as pl
from jax.experimental.pallas import tpu as pltpu
from jax.sharding import PartitionSpec as P

HEADS = 8
PER = 12
EPS = 1e-05
BF = jnp.bfloat16
F32 = jnp.float32
NT = (((1,), (1,)), ((), ()))
NN = (((1,), (0,)), ((), ()))
TN = (((0,), (0,)), ((), ()))
CHUNKS = 2
MIB = 1024 * 1024
LAYER_VMEM = 49 * MIB
COLLECT_VMEM = 52 * MIB
PARTS = 4
OWNERS = 16
GROUP = 16
COST = pl.CostEstimate(flops=12_000_000_000, bytes_accessed=20_000_000, transcendentals=0)
PARTS_ORDER = (2, 3, 1, 0)
STEP = 256


def dot(a, b, dims=NN):
    return lax.dot_general(a, b, dims, preferred_element_type=F32)


def iota(shape, dim):
    return lax.broadcasted_iota(jnp.int32, shape, dim)


def ids_kernel(order_hbm, ids_hbm, out_hbm, order, raw, ids_scr, out, sems):
    hashes, users, length = raw.shape
    owners = out.shape[0] // users
    get_order = pltpu.make_async_copy(order_hbm, order, sems.at[0])
    get_ids = pltpu.make_async_copy(ids_hbm, raw, sems.at[1])
    get_order.start()
    get_ids.start()
    ids_scr[...] = jnp.full(ids_scr.shape, -1, jnp.int32)
    get_order.wait()
    get_ids.wait()
    for b in range(users):
        user = order[b]
        for h in range(hashes):
            ids_scr[b : b + 1, h * length : (h + 1) * length] = raw[h, pl.ds(user, 1), :]
    ids = ids_scr[...]
    lanes = ids.shape[1]
    owner = lax.shift_right_arithmetic(ids, 10)
    hash_of = lax.div(iota(ids.shape, 1), length)
    code = (ids & 1023) + 1024 * hash_of
    high = (lax.shift_right_logical(code, 6)).astype(F32)
    low = (code & 63).astype(F32)
    hits = [jnp.where(owner == o, 1.0, 0.0).astype(F32) for o in range(owners)]
    before = jnp.where(iota((lanes, lanes), 0) < iota((lanes, lanes), 1), 1.0, 0.0).astype(BF)
    prefix = dot(jnp.concatenate(hits, axis=0).astype(BF), before)
    rank = jnp.zeros(ids.shape, F32)
    for o in range(owners):
        rank = rank + hits[o] * prefix[o * users : (o + 1) * users]
    rank = rank.astype(jnp.int32)
    total = jnp.zeros((2 * owners, 128), F32)
    for b in range(users):
        hit = iota((owners, lanes), 0) == owner[b : b + 1]
        left = jnp.concatenate(
            [jnp.where(hit, high[b : b + 1], 0.0), jnp.where(hit, low[b : b + 1], 0.0)], axis=0
        ).astype(BF)
        right = jnp.where(iota((128, lanes), 0) == rank[b : b + 1] + PER * b, 1.0, 0.0).astype(BF)
        total = total + dot(left, right, NT)
    codes = (total[:owners] * 64.0 + total[owners:]).astype(jnp.int32)
    slots = owner * 16 + rank
    for b in range(users):
        part = pl.ds(b * owners, owners)
        out[part, 0, :128] = codes
        out[part, 0, 128:] = jnp.broadcast_to(slots[b : b + 1], (owners, lanes))
    put = pltpu.make_async_copy(out, out_hbm, sems.at[2])
    put.start()
    put.wait()


def leaving_ids(order, ids, owners):
    hashes, users, length = ids.shape
    hbm = pl.BlockSpec(memory_space=pltpu.HBM)
    free = pl.BlockSpec(memory_space=pl.ANY)
    shape = (users * owners, 1, 384)
    return pl.pallas_call(
        ids_kernel,
        out_shape=jax.ShapeDtypeStruct(shape, jnp.int32),
        in_specs=[hbm, hbm],
        out_specs=free,
        scratch_shapes=[
            pltpu.SMEM((users,), jnp.int32),
            pltpu.VMEM(ids.shape, jnp.int32),
            pltpu.VMEM((users, 256), jnp.int32),
            pltpu.VMEM(shape, jnp.int32),
            pltpu.SemaphoreType.DMA((3,)),
        ],
        compiler_params=pltpu.CompilerParams(vmem_limit_bytes=60 * MIB),
        name="leaving_ids",
    )(order, ids)


def serve_kernel(got_hbm, table_hbm, *refs):
    outs, (codes, raw, wide, stages, out, sems) = refs[:CHUNKS], refs[CHUNKS:]
    hashes, rows, width = table_hbm.shape
    tiles = width // 128
    _, requesters, half, _ = out.shape
    half_users = half // PER
    parts = 2 * hashes
    size = rows // 2
    get_codes = pltpu.make_async_copy(got_hbm.at[:, 0, pl.ds(0, 128)], codes, sems.at[parts])
    places = [(i // 2, (i % 2) * size) for i in range(parts)]
    copies = [
        pltpu.make_async_copy(
            table_hbm.at[h, pl.ds(first, size)], raw.at[h, pl.ds(first, size)], sems.at[i]
        )
        for i, (h, first) in enumerate(places)
    ]
    copies[0].start()
    get_codes.start()
    for copy in copies[1:]:
        copy.start()
    for i, (h, first) in enumerate(places):
        copies[i].wait()

        @pl.loop(0, size // 64)
        def _(g):
            for q in range(4):
                at = pl.multiple_of(first + g * 64 + q * 16, 16)
                for c in range(tiles):
                    both = raw[h, pl.ds(at, 16), c * 128 : (c + 1) * 128].astype(F32)
                    base = (h * rows + at) * tiles + c
                    wide[pl.ds(base, 8, stride=tiles), :] = both[:8]
                    wide[pl.ds(base + 8 * tiles, 8, stride=tiles), :] = both[8:]

    get_codes.wait()
    first_lane = lax.axis_index("batch") * PER

    def gather(side, t, part):
        for j in range(half_users):
            home = (part * half_users + j) * requesters + t
            for k in range(PER):
                row = codes[home, first_lane + k]
                slot = (j * PER + k) * tiles
                stages[side, slot : slot + tiles, :] = wide[
                    pl.ds(pl.multiple_of(row * tiles, tiles), tiles), :
                ]

    def pack(side, t, part):
        for g in range(half // 16):
            for c in range(tiles):
                base = g * 16 * tiles + c
                upper = stages[side, pl.ds(base, 8, stride=tiles), :]
                lower = stages[side, pl.ds(base + 8 * tiles, 8, stride=tiles), :]
                out[part, t, g * 16 : (g + 1) * 16, c * 128 : (c + 1) * 128] = jnp.concatenate(
                    [upper, lower], axis=0
                ).astype(BF)

    gather(0, 0, 0)

    @pl.loop(0, requesters)
    def _(t):
        gather(1, t, 1)
        pack(0, t, 0)

        @pl.when(t + 1 < requesters)
        def _():
            gather(0, t + 1, 0)

        pack(1, t, 1)
        for i in range(CHUNKS):
            pltpu.make_async_copy(out.at[i, t], outs[i].at[t], sems.at[parts + 1 + i]).start()

    puts = [
        pltpu.make_async_copy(out.at[i], outs[i], sems.at[parts + 1 + i]) for i in range(CHUNKS)
    ]
    for put in puts:
        put.wait()


def serve_rows(got, tables, requesters, per_chunk):
    hashes, rows, width = tables.shape
    tiles = width // 128
    shape = (requesters, per_chunk, width)
    hbm = pl.BlockSpec(memory_space=pltpu.HBM)
    free = pl.BlockSpec(memory_space=pl.ANY)
    return pl.pallas_call(
        serve_kernel,
        out_shape=[jax.ShapeDtypeStruct(shape, BF)] * CHUNKS,
        in_specs=[free, hbm],
        out_specs=[free, hbm],
        scratch_shapes=[
            pltpu.SMEM((got.shape[0], 128), jnp.int32),
            pltpu.VMEM(tables.shape, BF),
            pltpu.VMEM((hashes * rows * tiles, 128), F32),
            pltpu.VMEM((2, per_chunk * tiles, 128), F32),
            pltpu.VMEM((CHUNKS, *shape), BF),
            pltpu.SemaphoreType.DMA((2 * hashes + 1 + CHUNKS,)),
        ],
        compiler_params=pltpu.CompilerParams(vmem_limit_bytes=60 * MIB),
        name="serve_rows",
    )(got, tables)


def sigmoid(z):
    return 0.5 + 0.5 * jnp.tanh(0.5 * z)


def layer_kernel(chunk, *refs):
    len_hbm, got_hbm, fetched, cot_hbm, w_in_hbm, w_out_hbm = refs[:6]
    enc_hbm, grad_hbm, *refs = refs[7:] if chunk else refs[6:]
    lengths, got, cot, enc, grads, w_in, w_out, x_s, n_s, gate_s, *refs = refs
    dsilu_s, qkv_s, mixed_s, s_s, w_s, dw_s, dz_s, mask_s, sems = refs
    users, length, width = cot.shape
    tokens = users * length
    head = width // HEADS
    owners, per_chunk, _ = fetched.shape
    halves = 1
    half_users = users // halves
    half_tokens = tokens // halves
    half_rows = per_chunk // halves
    half_slots = owners * half_rows
    pair = 2 * length
    mine = lax.axis_index("table")
    our_users = pl.ds(chunk * users, users)

    def fetch(i, src, dst):
        copy = pltpu.make_async_copy(src, dst, sems.at[i])
        copy.start()
        return copy

    get_len = fetch(0, len_hbm, lengths)
    get_slots = [
        fetch(1 + j, got_hbm.at[pl.ds((chunk * users + j) * owners + mine, 1)], got.at[pl.ds(j, 1)])
        for j in range(users)
    ]
    sem_at = 1 + users
    get_w = {
        c: fetch(
            sem_at + c, w_in_hbm.at[0, :, pl.ds(c * width, width)], w_in.at[:, pl.ds(c * width, width)]
        )
        for c in PARTS_ORDER
    }
    sem_at += 4
    get_w_out = fetch(sem_at, w_out_hbm.at[0], w_out)
    get_cot = fetch(sem_at + 1, cot_hbm.at[our_users], cot)
    sem_at += 2

    get_len.wait()
    for copy in get_slots:
        copy.wait()
    slot_rows, slot_cols = [], []
    for i in range(halves):
        rows_of = []
        for h in range(3):
            packed = jnp.concatenate(
                [
                    got[i * half_users + j, :, 128 + h * length : 128 + (h + 1) * length]
                    for j in range(half_users)
                ],
                axis=1,
            )
            rows_of.append(
                lax.shift_right_logical(packed, 4) * half_rows
                + lax.div(iota((1, half_tokens), 1), length) * PER
                + (packed & 15)
            )
        stacked = jnp.concatenate(rows_of + [jnp.zeros((5, half_tokens), jnp.int32)], axis=0)
        slot_rows.append(rows_of)
        slot_cols.append(stacked.astype(F32).T.astype(jnp.int32))
    picks = []
    for i in range(halves):
        lane = iota((half_tokens, half_slots), 1)
        pick = (lane == slot_cols[i][:, 0:1]) | (lane == slot_cols[i][:, 1:2])
        pick = pick | (lane == slot_cols[i][:, 2:3])
        picks.append(jnp.where(pick, 1.0, 0.0).astype(BF))

    token_user = lax.div(iota((tokens, 1), 0), length)
    token_pos = iota((tokens, 1), 0) - token_user * length
    token_len = jnp.zeros((tokens, 1), jnp.int32)
    for u in range(users):
        token_len = jnp.where(token_user == u, lengths[chunk * users + u], token_len)
    live = jnp.where(token_pos < token_len, 1.0, 0.0).astype(F32)
    key = iota((tokens, pair), 1)
    query = iota((tokens, pair), 0)
    same = lax.div(key, length) == lax.rem(lax.div(query, length), 2)
    causal = lax.rem(key, length) <= lax.rem(query, length)
    mask_s[...] = jnp.where(same & causal, 1.0, 0.0) * live

    for i in range(halves):
        rows = slice(i * half_tokens, (i + 1) * half_tokens)
        block = fetched[:, i * half_rows : (i + 1) * half_rows, :].reshape(half_slots, width)
        x_s[rows] = dot(picks[i], block).astype(BF).astype(F32)
    x = x_s[...]
    mean = jnp.mean(x, axis=1, keepdims=True)
    centered = x - mean
    rstd = lax.rsqrt(jnp.mean(centered * centered, axis=1, keepdims=True) + EPS)
    n_s[...] = (centered * rstd).astype(BF)

    step = STEP
    for c in PARTS_ORDER:
        get_w[c].wait()

        @pl.loop(0, width // step)
        def _(i, c=c):
            cols = pl.ds(pl.multiple_of(i * step, step), step)
            z = dot(n_s[...], w_in[:, pl.ds(pl.multiple_of(c * width + i * step, step), step)])
            sig = sigmoid(z)
            out = z * sig
            dsilu_s[c, :, cols] = sig + out * (1.0 - sig)
            if c == 0:
                gate_s[:, cols] = out
            else:
                qkv_s[c - 1, :, cols] = out.astype(BF)

    scale = head ** (-0.5)
    blocks = [
        (slice(p * pair, (p + 1) * pair), slice(h * head, (h + 1) * head))
        for h in range(HEADS)
        for p in range(tokens // pair)
    ]
    for at in blocks:
        s_s[at] = dot(qkv_s[(1, *at)], qkv_s[(2, *at)], NT)
    mask = mask_s[...]
    for h in range(HEADS):
        cols = slice(h * head, (h + 1) * head)
        s = s_s[:, cols] * scale
        sig = sigmoid(s)
        out = s * sig
        w_s[:, cols] = (out * mask).astype(BF)
        dw_s[:, cols] = (sig + out * (1.0 - sig)) * (mask * scale)
    for at in blocks:
        mixed_s[at] = dot(w_s[at], qkv_s[(0, *at)])

    mixed = mixed_s[...]
    mean2 = jnp.mean(mixed, axis=1, keepdims=True)
    centered2 = mixed - mean2
    rstd2 = lax.rsqrt(jnp.mean(centered2 * centered2, axis=1, keepdims=True) + EPS)
    hat = centered2 * rstd2
    gate = gate_s[...]
    gated = (hat * gate).astype(BF)
    get_w_out.wait()
    out = (x_s[...] + dot(gated, w_out[...])) * live
    enc[...] = out.astype(BF).reshape(users, length, width)
    send_enc = fetch(sem_at, enc, enc_hbm.at[our_users])
    sem_at += 1

    get_cot.wait()
    g = cot[...].reshape(tokens, width).astype(F32) * live
    dgated = dot(g.astype(BF), w_out[...], NT).astype(BF).astype(F32)
    dz_s[0] = (dgated * hat * dsilu_s[0]).astype(BF)
    dhat = dgated * gate
    dmixed = rstd2 * (
        dhat
        - jnp.mean(dhat, axis=1, keepdims=True)
        - hat * jnp.mean(dhat * hat, axis=1, keepdims=True)
    )
    n_s[...] = dmixed.astype(BF)
    for at in blocks:
        s_s[at] = dot(n_s[at], qkv_s[(0, *at)], NT)
    for at in blocks:
        dv = dot(w_s[at], n_s[at], TN).astype(BF).astype(F32)
        dz_s[(1, *at)] = (dv * dsilu_s[(1, *at)]).astype(BF)
    for h in range(HEADS):
        cols = slice(h * head, (h + 1) * head)
        w_s[:, cols] = (s_s[:, cols].astype(BF).astype(F32) * dw_s[:, cols]).astype(BF)
    for at in blocks:
        dq = dot(w_s[at], qkv_s[(2, *at)]).astype(BF).astype(F32)
        dz_s[(2, *at)] = (dq * dsilu_s[(2, *at)]).astype(BF)
    for at in blocks:
        dk = dot(w_s[at], qkv_s[(1, *at)], TN).astype(BF).astype(F32)
        dz_s[(3, *at)] = (dk * dsilu_s[(3, *at)]).astype(BF)

    @pl.loop(0, width // step)
    def _(i):
        cols = pl.ds(pl.multiple_of(i * step, step), step)
        dn = dot(dz_s[0], w_in[cols, :width], NT)
        for c in range(1, 4):
            dn = dn + dot(dz_s[c], w_in[cols, c * width : (c + 1) * width], NT)
        mixed_s[:, cols] = dn

    dn = mixed_s[...].astype(BF).astype(F32)
    xhat = (x_s[...] - mean) * rstd
    dx = rstd * (
        dn
        - jnp.mean(dn, axis=1, keepdims=True)
        - xhat * jnp.mean(dn * xhat, axis=1, keepdims=True)
    )
    n_s[...] = (dx + g).astype(BF)
    puts = []
    for i in range(halves):
        sub = iota((half_slots, half_tokens), 0)
        put = (sub == slot_rows[i][0]) | (sub == slot_rows[i][1]) | (sub == slot_rows[i][2])
        puts.append(jnp.where(put, 1.0, 0.0).astype(BF))
    ranks = grads.shape[0]
    copies = [send_enc]
    for b in range(0, ranks, 2):
        cols = slice(b * 128, (b + 2) * 128)
        for i in range(halves):
            rows = slice(i * half_tokens, (i + 1) * half_tokens)
            two = dot(puts[i], n_s[rows, cols]).astype(BF)
            for r in range(2):
                grads[b + r, :, i * half_rows : (i + 1) * half_rows, :] = two[
                    :, r * 128 : (r + 1) * 128
                ].reshape(owners, half_rows, 128)
        copies.append(fetch(sem_at, grads.at[pl.ds(b, 2)], grad_hbm.at[pl.ds(b, 2)]))
        sem_at += 1
    for copy in copies:
        copy.wait()


def layer(chunk, lengths, got, fetched, cot, w_in, w_out, batch_ranks, prev):
    owners, per_chunk, width = fetched.shape
    all_users, length, _ = cot.shape
    users = all_users // CHUNKS
    tokens = users * length
    ours = (users, length, width)
    grad_shape = (batch_ranks, owners, per_chunk, width // batch_ranks)
    hbm = pl.BlockSpec(memory_space=pltpu.HBM)
    free = pl.BlockSpec(memory_space=pl.ANY)
    vmem = pl.BlockSpec(memory_space=pltpu.VMEM)
    args = (lengths, got, fetched, cot, w_in, w_out) + ((prev,) if chunk else ())
    return pl.pallas_call(
        functools.partial(layer_kernel, chunk),
        out_shape=[
            jax.ShapeDtypeStruct(cot.shape, BF),
            jax.ShapeDtypeStruct(grad_shape, BF),
        ],
        in_specs=[hbm, free, vmem, hbm, hbm, hbm, hbm][: len(args)],
        out_specs=[hbm, hbm],
        input_output_aliases={6: 0} if chunk else {},
        scratch_shapes=[
            pltpu.SMEM((all_users,), jnp.int32),
            pltpu.VMEM((users, 1, got.shape[2]), jnp.int32),
            pltpu.VMEM(ours, BF),
            pltpu.VMEM(ours, BF),
            pltpu.VMEM(grad_shape, BF),
            pltpu.VMEM((width, 4 * width), BF),
            pltpu.VMEM((width, width), BF),
            pltpu.VMEM((tokens, width), F32),
            pltpu.VMEM((tokens, width), BF),
            pltpu.VMEM((tokens, width), F32),
            pltpu.VMEM((4, tokens, width), F32),
            pltpu.VMEM((3, tokens, width), BF),
            pltpu.VMEM((tokens, width), F32),
            pltpu.VMEM((tokens, width), F32),
            pltpu.VMEM((tokens, width), BF),
            pltpu.VMEM((tokens, width), F32),
            pltpu.VMEM((4, tokens, width), BF),
            pltpu.VMEM((tokens, 2 * length), F32),
            pltpu.SemaphoreType.DMA((10 + users + batch_ranks // 2,)),
        ],
        compiler_params=pltpu.CompilerParams(vmem_limit_bytes=LAYER_VMEM),
        cost_estimate=COST,
        name="layer",
    )(*args)


def collect_kernel(chunk, got_hbm, rows, *refs):
    prev_hbm = refs[0] if chunk else None
    out_hbm, got, codes, wide, hits, out, prev, sems = refs[1 if chunk else 0 :]
    senders, per_sender, cols = rows.shape
    ranks = senders // OWNERS
    users = per_sender // PER
    groups, depth = codes.shape
    group = senders // groups
    parts = wide.shape[1] // cols
    height = out.shape[0] // parts
    get_codes = pltpu.make_async_copy(got_hbm.at[:, :, pl.ds(0, 128)], got, sems.at[0])
    get_codes.start()
    if chunk:
        get_prev = pltpu.make_async_copy(prev_hbm, prev, sems.at[1])
        get_prev.start()
    get_codes.wait()
    if chunk:
        get_prev.wait()
    lane = iota((OWNERS, 128), 1)
    for b in range(ranks):
        line = jnp.zeros((OWNERS, 128), jnp.int32)
        for j in range(users):
            home = (chunk * users + j) * OWNERS
            block = got[home : home + OWNERS, 0, :]
            moved = pltpu.roll(block, ((j - b) * PER) % 128, 1)
            line = jnp.where((lane >= j * PER) & (lane < (j + 1) * PER), moved, line)
        for t in range(OWNERS):
            sender = b * OWNERS + t
            first = (sender % group) * per_sender
            codes[sender // group : sender // group + 1, first : first + per_sender] = line[
                t : t + 1, :per_sender
            ]
    part_cols = lax.div(codes[...], height).astype(F32).T.astype(jnp.int32)
    for s in range(groups):
        inside = lax.rem(codes[s : s + 1, :], height)
        for q in range(height // 128):
            near = jnp.clip(inside - 128 * q, -1, 128).astype(F32).astype(BF)
            row = iota((128, depth), 0).astype(F32).astype(BF)
            hits[q * 128 : (q + 1) * 128, s * depth : (s + 1) * depth] = jnp.where(
                row == near, jnp.ones((), BF), jnp.zeros((), BF)
            )
        block = rows[s * group : (s + 1) * group].reshape(depth, cols)
        for p in range(parts):
            here = part_cols[:, s : s + 1] == p
            wide[s * depth : (s + 1) * depth, p * cols : (p + 1) * cols] = jnp.where(
                here, block, jnp.zeros_like(block)
            )
    acc = dot(hits[...], wide[...])
    puts = []
    for p in range(parts):
        at = slice(p * height, (p + 1) * height)
        part = acc[:, p * cols : (p + 1) * cols]
        out[at, :] = part + prev[at, :] if chunk else part
        puts.append(pltpu.make_async_copy(out.at[at], out_hbm.at[at], sems.at[2 + p]))
        puts[-1].start()
    for put in puts:
        put.wait()


def collect(chunk, got, rows, prev, total):
    args = (got, rows) + ((prev,) if chunk else ())
    senders, per_sender, cols = rows.shape
    hbm = pl.BlockSpec(memory_space=pltpu.HBM)
    free = pl.BlockSpec(memory_space=pl.ANY)
    vmem = pl.BlockSpec(memory_space=pltpu.VMEM)
    return pl.pallas_call(
        functools.partial(collect_kernel, chunk),
        out_shape=jax.ShapeDtypeStruct((total, cols), F32),
        in_specs=[free, vmem, hbm][: len(args)],
        out_specs=hbm,
        scratch_shapes=[
            pltpu.VMEM((got.shape[0], 1, 128), jnp.int32),
            pltpu.VMEM((senders // GROUP, GROUP * per_sender), jnp.int32),
            pltpu.VMEM((senders * per_sender, PARTS * cols), BF),
            pltpu.VMEM((total // PARTS, senders * per_sender), BF),
            pltpu.VMEM((total, cols), F32),
            pltpu.VMEM((total, cols), F32),
            pltpu.SemaphoreType.DMA((2 + PARTS,)),
        ],
        compiler_params=pltpu.CompilerParams(vmem_limit_bytes=COLLECT_VMEM),
        cost_estimate=COST,
        name="collect",
    )(*args)


def body(item_rows, send_order, user_lengths, tables, w_in, w_out, out_grad):
    batch_ranks = lax.axis_size("batch")
    table_ranks = lax.axis_size("table")
    users, length, hashes = item_rows.shape
    rows_local = tables.shape[1]
    both = ("batch", "table")
    per_chunk = users // CHUNKS * PER

    leaving = leaving_ids(send_order, item_rows.transpose(2, 0, 1), table_ranks)
    got = lax.all_to_all(leaving, both, 0, 0, tiled=True)
    served = serve_rows(got, tables, table_ranks, per_chunk)
    encoded, total, returned = None, None, []
    for c in range(CHUNKS):
        fetched = lax.all_to_all(served[c], "table", 0, 0, tiled=True)
        encoded, grads = layer(
            c, user_lengths, got, fetched, out_grad, w_in, w_out, batch_ranks, encoded
        )
        grads = grads.reshape(batch_ranks * table_ranks, per_chunk, -1)
        returned.append(lax.all_to_all(grads, both, 0, 0, tiled=True))
    for c in range(CHUNKS):
        total = collect(c, got, returned[c], total, hashes * rows_local)
    return encoded, total.reshape(hashes, rows_local, -1)


def solution(mesh):
    in_specs = (
        P(("batch", "table"), None, None),
        P(("batch", "table")),
        P(("batch", "table")),
        P(None, "table", None),
        P(),
        P(),
        P(("batch", "table"), None, None),
    )
    out_specs = (P(("batch", "table"), None, None), P(None, "table", "batch"))
    return jax.shard_map(body, mesh=mesh, in_specs=in_specs, out_specs=out_specs, check_vma=False)
```

profile of v0, /device:TPU:1, one launch (start us, length us, event | category | flops | bytes accessed | tf_op | source)
XLA Modules:
  0.0 153.4 jit_solution(10134424593442379694)
XLA Ops:
  0.6 2.0 %leaving_ids.1 = s32[128,1,384]{2,1,0:T(1,128)} custom-call(s32[8]{0:T(128)} %order_hbm.1, s32[3,8,64]{2,1,0:T(8,128)} %bitcast.4), custom_call_target="tpu_custom_call" | custom-call | tf_op jit(solution)/shard_map/leaving_ids/pallas_call | solution.py:90
  2.7 22.2 %all_to_all.25.got_hbm.refs_1_ = s32[128,1,384]{2,1,0:T(1,128)} all-to-all(s32[128,1,384]{2,1,0:T(1,128)} %leaving_ids.1), channel_id=1, replica_groups=mesh['batch'=8,'table'=16] {'batch','table'}, dimensions={0} | all-to-all | bytes 393216 | tf_op jit(solution)/shard_map/all_to_all | solution.py:557
  24.9 7.9 %serve_rows.1 = (bf16[16,48,1024]{2,1,0:T(8,128)(2,1)}, bf16[16,48,1024]{2,1,0:T(8,128)(2,1)}) custom-call(s32[128,1,384]{2,1,0:T(1,128)} %all_to_all.25.got_hbm.refs_1_, bf16[3,1024,1024]{2,1,0:T(8,128)(2,1)} %table_hbm.1), custom_call_target="tpu_custom_call" | custom-call | tf_op jit(solution)/shard_map/serve_rows/pallas_call | solution.py:191
  32.8 25.6 %all_to_all.26.refs_2_ = bf16[16,48,1024]{2,1,0:T(8,128)(2,1)S(1)} all-to-all(bf16[16,48,1024]{2,1,0:T(8,128)(2,1)} %get-tuple-element.9), channel_id=1, replica_groups=mesh['batch'=8,'table'=16] {'table'}, dimensions={0} | all-to-all | bytes 3145728 | tf_op jit(solution)/shard_map/all_to_all | solution.py:561
  58.4 0.0 copy-start
  58.4 0.0 copy-start.3
  58.4 3.8 %all-to-all-start.1 = ((bf16[16,48,1024]{2,1,0:T(8,128)(2,1)}), bf16[16,48,1024]{2,1,0:T(8,128)(2,1)S(1)}, u32[]{:S(2)}, u32[]{:S(2)}) async-start(bf16[16,48,1024]{2,1,0:T(8,128)(2,1)} %get-tuple-element.8), calls=%async_computation.1 | async-start | bytes 3145728 | tf_op jit(solution)/shard_map/all_to_all | solution.py:561
  62.3 0.0 copy-done
  62.3 0.0 copy-done.3
  62.3 0.0 copy-start.1
  62.3 1.2 copy-done.1
  63.5 16.6 %layer.2 = (bf16[8,64,1024]{2,1,0:T(8,128)(2,1)}, bf16[8,16,48,128]{3,2,1,0:T(8,128)(2,1)}) custom-call(s32[8]{0:T(128)S(1)} %copy-done.3, s32[128,1,384]{2,1,0:T(1,128)S(1)} %copy-done, bf16[16,48,1024]{2,1,0:T(8,128)(2,1)S(1)} %all_to_all.26.refs_2_, bf16[8,64,1024]{2,1,0:T(8,128)(2,1)S(1)} %copy-done.1, bf16[1,1024,4096]{2,1,0:T(8,128)(2,1)} %refs_4_.3, ...), custom_call_target="tpu_custom_call" | custom-call | flops 12000000000 | bytes 20000000 | tf_op jit(solution)/shard_map/layer/pallas_call | solution.py:427
  80.1 2.9 %all-to-all-done.1.refs_2_ = bf16[16,48,1024]{2,1,0:T(8,128)(2,1)S(1)} async-done(((bf16[16,48,1024]{2,1,0:T(8,128)(2,1)}), bf16[16,48,1024]{2,1,0:T(8,128)(2,1)S(1)}, u32[]{:S(2)}, u32[]{:S(2)}) %all-to-all-start.1) | async-done | bytes 1572896 | tf_op jit(solution)/shard_map/all_to_all | solution.py:561
  83.0 0.0 copy-start.2
  83.0 8.4 %all-to-all-start.4 = ((bf16[128,48,128]{2,1,0:T(8,128)(2,1)}), bf16[128,48,128]{2,1,0:T(8,128)(2,1)}, u32[]{:S(2)}, u32[]{:S(2)}) async-start(bf16[128,48,128]{2,1,0:T(8,128)(2,1)} %bitcast.2), calls=%async_computation.4 | async-start | bytes 3145728 | tf_op jit(solution)/shard_map/all_to_all | solution.py:566
  91.4 0.0 copy-done.2
  91.5 16.6 %layer.3 = (bf16[8,64,1024]{2,1,0:T(8,128)(2,1)}, bf16[8,16,48,128]{3,2,1,0:T(8,128)(2,1)}) custom-call(s32[8]{0:T(128)S(1)} %copy-done.3, s32[128,1,384]{2,1,0:T(1,128)S(1)} %copy-done, bf16[16,48,1024]{2,1,0:T(8,128)(2,1)S(1)} %all-to-all-done.1.refs_2_, bf16[8,64,1024]{2,1,0:T(8,128)(2,1)S(1)} %copy-done.2, ...), custom_call_target="tpu_custom_call", output_to_operand_aliasing={{0}: (6, {})} | custom-call | flops 12000000000 | bytes 20000000 | tf_op jit(solution)/shard_map/layer/pallas_call | solution.py:427
  108.1 7.3 %all-to-all-done.4.rows = bf16[128,48,128]{2,1,0:T(8,128)(2,1)} async-done(((bf16[128,48,128]{2,1,0:T(8,128)(2,1)}), bf16[128,48,128]{2,1,0:T(8,128)(2,1)}, u32[]{:S(2)}, u32[]{:S(2)}) %all-to-all-start.4) | async-done | bytes 1572896 | tf_op jit(solution)/shard_map/all_to_all | solution.py:566
  115.4 4.8 %all-to-all-start.3 = ((bf16[128,48,128]{2,1,0:T(8,128)(2,1)}), bf16[128,48,128]{2,1,0:T(8,128)(2,1)S(1)}, u32[]{:S(2)}, u32[]{:S(2)}) async-start(bf16[128,48,128]{2,1,0:T(8,128)(2,1)} %bitcast.1), calls=%async_computation.3 | async-start | bytes 3145728 | tf_op jit(solution)/shard_map/all_to_all | solution.py:566
  120.2 8.7 %collect.2.refs_0_ = f32[3072,128]{1,0:T(8,128)S(1)} custom-call(s32[128,1,384]{2,1,0:T(1,128)S(1)} %copy-done, bf16[128,48,128]{2,1,0:T(8,128)(2,1)} %all-to-all-done.4.rows), custom_call_target="tpu_custom_call" | custom-call | flops 12000000000 | bytes 20000000 | tf_op jit(solution)/shard_map/collect/pallas_call | solution.py:528
  128.9 0.0 copy-start.4
  128.9 1.1 copy-done.4
  130.1 14.4 %all-to-all-done.3.rows = bf16[128,48,128]{2,1,0:T(8,128)(2,1)S(1)} async-done(((bf16[128,48,128]{2,1,0:T(8,128)(2,1)}), bf16[128,48,128]{2,1,0:T(8,128)(2,1)S(1)}, u32[]{:S(2)}, u32[]{:S(2)}) %all-to-all-start.3) | async-done | bytes 1572896 | tf_op jit(solution)/shard_map/all_to_all | solution.py:566
  144.5 8.8 %collect.3 = f32[3072,128]{1,0:T(8,128)} custom-call(s32[128,1,384]{2,1,0:T(1,128)S(1)} %copy-done, bf16[128,48,128]{2,1,0:T(8,128)(2,1)S(1)} %all-to-all-done.3.rows, f32[3072,128]{1,0:T(8,128)} %copy-done.4), custom_call_target="tpu_custom_call" | custom-call | flops 12000000000 | bytes 20000000 | tf_op jit(solution)/shard_map/collect/pallas_call | solution.py:528
Async XLA Ops:
  58.4 3.9 %copy-start = (s32[128,1,384]{2,1,0:T(1,128)S(1)}, s32[128,1,384]{2,1,0:T(1,128)}, u32[]{:S(2)}) copy-start(s32[128,1,384]{2,1,0:T(1,128)} %all_to_all.25.got_hbm.refs_1_) | copy-start | bytes 589828
  58.4 3.9 %copy-start.3 = (s32[8]{0:T(128)S(1)}, s32[8]{0:T(128)}, u32[]{:S(2)}) copy-start(s32[8]{0:T(128)} %refs_0_.3) | copy-start | bytes 100
  58.4 24.6 %all-to-all-start.1 = ((bf16[16,48,1024]{2,1,0:T(8,128)(2,1)}), bf16[16,48,1024]{2,1,0:T(8,128)(2,1)S(1)}, u32[]{:S(2)}, u32[]{:S(2)}) async-start(bf16[16,48,1024]{2,1,0:T(8,128)(2,1)} %get-tuple-element.8), calls=%async_computation.1 | async-start | bytes 3145728 | tf_op jit(solution)/shard_map/all_to_all | solution.py:561
  62.3 1.2 copy-start.1
  83.0 8.4 %copy-start.2 = (bf16[8,64,1024]{2,1,0:T(8,128)(2,1)S(1)}, bf16[8,64,1024]{2,1,0:T(8,128)(2,1)}, u32[]{:S(2)}) copy-start(bf16[8,64,1024]{2,1,0:T(8,128)(2,1)} %refs_3_.3) | copy-start | bytes 3145732
  83.0 32.4 %all-to-all-start.4 = ((bf16[128,48,128]{2,1,0:T(8,128)(2,1)}), bf16[128,48,128]{2,1,0:T(8,128)(2,1)}, u32[]{:S(2)}, u32[]{:S(2)}) async-start(bf16[128,48,128]{2,1,0:T(8,128)(2,1)} %bitcast.2), calls=%async_computation.4 | async-start | bytes 3145728 | tf_op jit(solution)/shard_map/all_to_all | solution.py:566
  115.4 29.1 %all-to-all-start.3 = ((bf16[128,48,128]{2,1,0:T(8,128)(2,1)}), bf16[128,48,128]{2,1,0:T(8,128)(2,1)S(1)}, u32[]{:S(2)}, u32[]{:S(2)}) async-start(bf16[128,48,128]{2,1,0:T(8,128)(2,1)} %bitcast.1), calls=%async_computation.3 | async-start | bytes 3145728 | tf_op jit(solution)/shard_map/all_to_all | solution.py:566
  128.9 1.1 copy-start.4
where the time goes:
time: 154 us; the launch traced here: 153 us
  Pallas kernels  60.6 us (39%)
  blocking collectives  47.8 us (31%)
  waiting for transfers between devices  24.6 us (16%)
  starting transfers between devices  17.1 us (11%)
  local copies, waits for them, and re-layouts  2.37 us (2%)
    pallas_call x2, Pallas kernels, layer(): pl.pallas_call(functools.partial(layer_kernel, chunk), out_shape=[jax.Sha...  33.2 us
    all_to_all x1, blocking collectives, body(): fetched = lax.all_to_all(served[c], 'table', 0, 0, tiled=True)  25.6 us
    all_to_all x1, blocking collectives, body(): got = lax.all_to_all(leaving, both, 0, 0, tiled=True)  22.2 us
    all_to_all x2, waiting for transfers between devices, body(): returned.append(lax.all_to_all(grads, both, 0, 0, tiled=True))  21.7 us
    pallas_call x2, Pallas kernels, collect(): pl.pallas_call(functools.partial(collect_kernel, chunk), out_shape=jax.Sh...  17.5 us
    all_to_all x2, starting transfers between devices, body(): returned.append(lax.all_to_all(grads, both, 0, 0, tiled=True))  13.3 us
    pallas_call x1, Pallas kernels, serve_rows(): pl.pallas_call(serve_kernel, out_shape=[jax.ShapeDtypeStruct(shape, BF)]...  7.93 us
    all_to_all x1, starting transfers between devices, body(): fetched = lax.all_to_all(served[c], 'table', 0, 0, tiled=True)  3.84 us
  transfers between devices with their start and end apart: 3, of which 3 were waited for; matrix products, arithmetic and copies ran while one was open for 0% of the time, Pallas kernels for 27%

commit v1 on v0

--- a/solution.py
+++ b/solution.py
@@ -18,6 +18,7 @@
 CHUNKS = 2
 MIB = 1024 * 1024
 LAYER_VMEM = 49 * MIB
+SERVE_VMEM = 50 * MIB
 COLLECT_VMEM = 52 * MIB
 PARTS = 4
 OWNERS = 16
@@ -104,11 +105,11 @@
     )(order, ids)
 
 
-def serve_kernel(got_hbm, table_hbm, *refs):
-    outs, (codes, raw, wide, stages, out, sems) = refs[:CHUNKS], refs[CHUNKS:]
+def serve_kernel(got_hbm, table_hbm, first_out, second_hbm, codes, raw, wide, stages, second, sems):
+    outs = (first_out, second)
     hashes, rows, width = table_hbm.shape
     tiles = width // 128
-    _, requesters, half, _ = out.shape
+    requesters, half, _ = second.shape
     half_users = half // PER
     parts = 2 * hashes
     size = rows // 2
@@ -156,7 +157,7 @@
                 base = g * 16 * tiles + c
                 upper = stages[side, pl.ds(base, 8, stride=tiles), :]
                 lower = stages[side, pl.ds(base + 8 * tiles, 8, stride=tiles), :]
-                out[part, t, g * 16 : (g + 1) * 16, c * 128 : (c + 1) * 128] = jnp.concatenate(
+                outs[part][t, g * 16 : (g + 1) * 16, c * 128 : (c + 1) * 128] = jnp.concatenate(
                     [upper, lower], axis=0
                 ).astype(BF)
 
@@ -172,14 +173,9 @@
             gather(0, t + 1, 0)
 
         pack(1, t, 1)
-        for i in range(CHUNKS):
-            pltpu.make_async_copy(out.at[i, t], outs[i].at[t], sems.at[parts + 1 + i]).start()
-
-    puts = [
-        pltpu.make_async_copy(out.at[i], outs[i], sems.at[parts + 1 + i]) for i in range(CHUNKS)
-    ]
-    for put in puts:
-        put.wait()
+        pltpu.make_async_copy(second.at[t], second_hbm.at[t], sems.at[parts + 1]).start()
+
+    pltpu.make_async_copy(second, second_hbm, sems.at[parts + 1]).wait()
 
 
 def serve_rows(got, tables, requesters, per_chunk):
@@ -192,16 +188,16 @@
         serve_kernel,
         out_shape=[jax.ShapeDtypeStruct(shape, BF)] * CHUNKS,
         in_specs=[free, hbm],
-        out_specs=[free, hbm],
+        out_specs=[pl.BlockSpec(memory_space=pltpu.VMEM), hbm],
         scratch_shapes=[
             pltpu.SMEM((got.shape[0], 128), jnp.int32),
             pltpu.VMEM(tables.shape, BF),
             pltpu.VMEM((hashes * rows * tiles, 128), F32),
             pltpu.VMEM((2, per_chunk * tiles, 128), F32),
-            pltpu.VMEM((CHUNKS, *shape), BF),
-            pltpu.SemaphoreType.DMA((2 * hashes + 1 + CHUNKS,)),
+            pltpu.VMEM(shape, BF),
+            pltpu.SemaphoreType.DMA((2 * hashes + 2,)),
         ],
-        compiler_params=pltpu.CompilerParams(vmem_limit_bytes=60 * MIB),
+        compiler_params=pltpu.CompilerParams(vmem_limit_bytes=SERVE_VMEM),
         name="serve_rows",
     )(got, tables)
 
@@ -460,31 +456,15 @@
     )(*args)
 
 
-def collect_kernel(chunk, got_hbm, rows, *refs):
-    prev_hbm = refs[0] if chunk else None
-    out_hbm, got, codes, wide, hits, out, prev, sems = refs[1 if chunk else 0 :]
-    senders, per_sender, cols = rows.shape
-    ranks = senders // OWNERS
+def arrange(chunk, got, codes, per_sender):
+    group = codes.shape[1] // per_sender
     users = per_sender // PER
-    groups, depth = codes.shape
-    group = senders // groups
-    parts = wide.shape[1] // cols
-    height = out.shape[0] // parts
-    get_codes = pltpu.make_async_copy(got_hbm.at[:, :, pl.ds(0, 128)], got, sems.at[0])
-    get_codes.start()
-    if chunk:
-        get_prev = pltpu.make_async_copy(prev_hbm, prev, sems.at[1])
-        get_prev.start()
-    get_codes.wait()
-    if chunk:
-        get_prev.wait()
     lane = iota((OWNERS, 128), 1)
-    for b in range(ranks):
+    for b in range(got.shape[0] // OWNERS):
         line = jnp.zeros((OWNERS, 128), jnp.int32)
         for j in range(users):
             home = (chunk * users + j) * OWNERS
-            block = got[home : home + OWNERS, 0, :]
-            moved = pltpu.roll(block, ((j - b) * PER) % 128, 1)
+            moved = pltpu.roll(got[home : home + OWNERS, 0, :], ((j - b) * PER) % 128, 1)
             line = jnp.where((lane >= j * PER) & (lane < (j + 1) * PER), moved, line)
         for t in range(OWNERS):
             sender = b * OWNERS + t
@@ -492,6 +472,30 @@
             codes[sender // group : sender // group + 1, first : first + per_sender] = line[
                 t : t + 1, :per_sender
             ]
+
+
+def collect_kernel(chunk, given, rows, *refs):
+    if chunk:
+        prev_hbm, out_hbm, codes, wide, hits, out, prev, sems = refs
+    else:
+        out_hbm, next_hbm, got, codes, later, wide, hits, out, sems = refs
+    senders, per_sender, cols = rows.shape
+    groups, depth = codes.shape
+    group = senders // groups
+    parts = wide.shape[1] // cols
+    height = out.shape[0] // parts
+    if chunk:
+        get_codes = pltpu.make_async_copy(given, codes, sems.at[0])
+        get_prev = pltpu.make_async_copy(prev_hbm, prev, sems.at[1])
+        get_codes.start()
+        get_prev.start()
+        get_codes.wait()
+        get_prev.wait()
+    else:
+        get_ids = pltpu.make_async_copy(given.at[:, :, pl.ds(0, 128)], got, sems.at[0])
+        get_ids.start()
+        get_ids.wait()
+        arrange(0, got, codes, per_sender)
     part_cols = lax.div(codes[...], height).astype(F32).T.astype(jnp.int32)
     for s in range(groups):
         inside = lax.rem(codes[s : s + 1, :], height)
@@ -515,34 +519,41 @@
         out[at, :] = part + prev[at, :] if chunk else part
         puts.append(pltpu.make_async_copy(out.at[at], out_hbm.at[at], sems.at[2 + p]))
         puts[-1].start()
+    if not chunk:
+        arrange(1, got, later, per_sender)
+        puts.append(pltpu.make_async_copy(later, next_hbm, sems.at[1]))
+        puts[-1].start()
     for put in puts:
         put.wait()
 
 
-def collect(chunk, got, rows, prev, total):
-    args = (got, rows) + ((prev,) if chunk else ())
+def collect(chunk, given, rows, prev, total):
     senders, per_sender, cols = rows.shape
     hbm = pl.BlockSpec(memory_space=pltpu.HBM)
     free = pl.BlockSpec(memory_space=pl.ANY)
     vmem = pl.BlockSpec(memory_space=pltpu.VMEM)
+    code_shape = (senders // GROUP, GROUP * per_sender)
+    result = jax.ShapeDtypeStruct((total, cols), F32)
+    ordered = pltpu.VMEM(code_shape, jnp.int32)
+    before = [] if chunk else [pltpu.VMEM((given.shape[0], 1, 128), jnp.int32)]
     return pl.pallas_call(
         functools.partial(collect_kernel, chunk),
-        out_shape=jax.ShapeDtypeStruct((total, cols), F32),
-        in_specs=[free, vmem, hbm][: len(args)],
-        out_specs=hbm,
-        scratch_shapes=[
-            pltpu.VMEM((got.shape[0], 1, 128), jnp.int32),
-            pltpu.VMEM((senders // GROUP, GROUP * per_sender), jnp.int32),
+        out_shape=result if chunk else [result, jax.ShapeDtypeStruct(code_shape, jnp.int32)],
+        in_specs=[free, vmem, hbm] if chunk else [free, vmem],
+        out_specs=hbm if chunk else [hbm, hbm],
+        scratch_shapes=before
+        + [ordered] * (1 if chunk else 2)
+        + [
             pltpu.VMEM((senders * per_sender, PARTS * cols), BF),
             pltpu.VMEM((total // PARTS, senders * per_sender), BF),
             pltpu.VMEM((total, cols), F32),
-            pltpu.VMEM((total, cols), F32),
-            pltpu.SemaphoreType.DMA((2 + PARTS,)),
-        ],
+        ]
+        + ([pltpu.VMEM((total, cols), F32)] if chunk else [])
+        + [pltpu.SemaphoreType.DMA((2 + PARTS,))],
         compiler_params=pltpu.CompilerParams(vmem_limit_bytes=COLLECT_VMEM),
         cost_estimate=COST,
         name="collect",
-    )(*args)
+    )(*((given, rows, prev) if chunk else (given, rows)))
 
 
 def body(item_rows, send_order, user_lengths, tables, w_in, w_out, out_grad):
@@ -556,7 +567,7 @@
     leaving = leaving_ids(send_order, item_rows.transpose(2, 0, 1), table_ranks)
     got = lax.all_to_all(leaving, both, 0, 0, tiled=True)
     served = serve_rows(got, tables, table_ranks, per_chunk)
-    encoded, total, returned = None, None, []
+    encoded, returned = None, []
     for c in range(CHUNKS):
         fetched = lax.all_to_all(served[c], "table", 0, 0, tiled=True)
         encoded, grads = layer(
@@ -564,8 +575,8 @@
         )
         grads = grads.reshape(batch_ranks * table_ranks, per_chunk, -1)
         returned.append(lax.all_to_all(grads, both, 0, 0, tiled=True))
-    for c in range(CHUNKS):
-        total = collect(c, got, returned[c], total, hashes * rows_local)
+    total, codes = collect(0, got, returned[0], None, hashes * rows_local)
+    total = collect(1, codes, returned[1], total, hashes * rows_local)
     return encoded, total.reshape(hashes, rows_local, -1)
 
 

time: 154 us -> 152 us (0.987)
  transfers between devices with their start and end apart: 3 -> 3, of which waited for: 3 -> 3; matrix products, arithmetic and copies ran while one was open for 0% -> 0% of each run, Pallas kernels for 27% -> 28%
where the time goes in v1:
time: 152 us; the launch traced here: 151 us
  Pallas kernels  60.3 us (40%)
  blocking collectives  46.5 us (31%)
  waiting for transfers between devices  23.9 us (16%)
  starting transfers between devices  17.2 us (11%)
  local copies, waits for them, and re-layouts  2.38 us (2%)
    pallas_call x2, Pallas kernels, layer(): pl.pallas_call(functools.partial(layer_kernel, chunk), out_shape=[jax.Sha...  33.2 us
    all_to_all x1, blocking collectives, body(): fetched = lax.all_to_all(served[c], 'table', 0, 0, tiled=True)  24.4 us
    all_to_all x1, blocking collectives, body(): got = lax.all_to_all(leaving, both, 0, 0, tiled=True)  22.1 us
    all_to_all x2, waiting for transfers between devices, body(): returned.append(lax.all_to_all(grads, both, 0, 0, tiled=True))  21.2 us
    pallas_call x2, Pallas kernels, collect(): pl.pallas_call(functools.partial(collect_kernel, chunk), out_shape=result...  17.2 us
    all_to_all x2, starting transfers between devices, body(): returned.append(lax.all_to_all(grads, both, 0, 0, tiled=True))  13.4 us
    pallas_call x1, Pallas kernels, serve_rows(): pl.pallas_call(serve_kernel, out_shape=[jax.ShapeDtypeStruct(shape, BF)]...  7.9 us
    all_to_all x1, starting transfers between devices, body(): fetched = lax.all_to_all(served[c], 'table', 0, 0, tiled=True)  3.84 us
  transfers between devices with their start and end apart: 3, of which 3 were waited for; matrix products, arithmetic and copies ran while one was open for 0% of the time, Pallas kernels for 28%

profile of v1, /device:TPU:1, one launch (start us, length us, event | category | flops | bytes accessed | tf_op | source)
XLA Modules:
  0.0 151.2 jit_solution(9728921970388489924)
XLA Ops:
  0.6 2.0 %leaving_ids.1 = s32[128,1,384]{2,1,0:T(1,128)} custom-call(s32[8]{0:T(128)} %order_hbm.1, s32[3,8,64]{2,1,0:T(8,128)} %bitcast.4), custom_call_target="tpu_custom_call" | custom-call | tf_op jit(solution)/shard_map/leaving_ids/pallas_call | solution.py:91
  2.7 22.1 %all_to_all.25.got_hbm.refs_1_.given = s32[128,1,384]{2,1,0:T(1,128)S(1)} all-to-all(s32[128,1,384]{2,1,0:T(1,128)} %leaving_ids.1), channel_id=1, replica_groups=mesh['batch'=8,'table'=16] {'batch','table'}, dimensions={0} | all-to-all | bytes 393216 | tf_op jit(solution)/shard_map/all_to_all | solution.py:568
  24.8 7.9 %serve_rows.1 = (bf16[16,48,1024]{2,1,0:T(8,128)(2,1)S(1)}, bf16[16,48,1024]{2,1,0:T(8,128)(2,1)}) custom-call(s32[128,1,384]{2,1,0:T(1,128)S(1)} %all_to_all.25.got_hbm.refs_1_.given, bf16[3,1024,1024]{2,1,0:T(8,128)(2,1)} %table_hbm.1), custom_call_target="tpu_custom_call" | custom-call | tf_op jit(solution)/shard_map/serve_rows/pallas_call | solution.py:187
  32.7 24.4 %all_to_all.26.refs_2_ = bf16[16,48,1024]{2,1,0:T(8,128)(2,1)S(1)} all-to-all(bf16[16,48,1024]{2,1,0:T(8,128)(2,1)S(1)} %get-tuple-element.11), channel_id=1, replica_groups=mesh['batch'=8,'table'=16] {'table'}, dimensions={0} | all-to-all | bytes 3145728 | tf_op jit(solution)/shard_map/all_to_all | solution.py:572
  57.1 0.0 copy-start.2
  57.1 3.8 %all-to-all-start.1 = ((bf16[16,48,1024]{2,1,0:T(8,128)(2,1)}), bf16[16,48,1024]{2,1,0:T(8,128)(2,1)S(1)}, u32[]{:S(2)}, u32[]{:S(2)}) async-start(bf16[16,48,1024]{2,1,0:T(8,128)(2,1)} %get-tuple-element.10), calls=%async_computation.1 | async-start | bytes 3145728 | tf_op jit(solution)/shard_map/all_to_all | solution.py:572
  60.9 0.0 copy-done.2
  60.9 0.0 copy-start
  60.9 1.2 copy-done
  62.1 16.6 %layer.2 = (bf16[8,64,1024]{2,1,0:T(8,128)(2,1)}, bf16[8,16,48,128]{3,2,1,0:T(8,128)(2,1)}) custom-call(s32[8]{0:T(128)S(1)} %copy-done.2, s32[128,1,384]{2,1,0:T(1,128)S(1)} %all_to_all.25.got_hbm.refs_1_.given, bf16[16,48,1024]{2,1,0:T(8,128)(2,1)S(1)} %all_to_all.26.refs_2_, bf16[8,64,1024]{2,1,0:T(8,128)(2,1)S(1)} %copy-done, ...), custom_call_target="tpu_custom_call" | custom-call | flops 12000000000 | bytes 20000000 | tf_op jit(solution)/shard_map/layer/pallas_call | solution.py:423
  78.7 2.7 %all-to-all-done.1.refs_2_ = bf16[16,48,1024]{2,1,0:T(8,128)(2,1)S(1)} async-done(((bf16[16,48,1024]{2,1,0:T(8,128)(2,1)}), bf16[16,48,1024]{2,1,0:T(8,128)(2,1)S(1)}, u32[]{:S(2)}, u32[]{:S(2)}) %all-to-all-start.1) | async-done | bytes 1572896 | tf_op jit(solution)/shard_map/all_to_all | solution.py:572
  81.4 0.0 copy-start.1
  81.4 8.5 %all-to-all-start.3 = ((bf16[128,48,128]{2,1,0:T(8,128)(2,1)}), bf16[128,48,128]{2,1,0:T(8,128)(2,1)}, u32[]{:S(2)}, u32[]{:S(2)}) async-start(bf16[128,48,128]{2,1,0:T(8,128)(2,1)} %bitcast.1), calls=%async_computation.3 | async-start | bytes 3145728 | tf_op jit(solution)/shard_map/all_to_all | solution.py:577
  90.0 0.0 copy-done.1
  90.0 16.6 %layer.3 = (bf16[8,64,1024]{2,1,0:T(8,128)(2,1)}, bf16[8,16,48,128]{3,2,1,0:T(8,128)(2,1)}) custom-call(s32[8]{0:T(128)S(1)} %copy-done.2, s32[128,1,384]{2,1,0:T(1,128)S(1)} %all_to_all.25.got_hbm.refs_1_.given, bf16[16,48,1024]{2,1,0:T(8,128)(2,1)S(1)} %all-to-all-done.1.refs_2_, ...), custom_call_target="tpu_custom_call", output_to_operand_aliasing={{0}: (6, {})} | custom-call | flops 12000000000 | bytes 20000000 | tf_op jit(solution)/shard_map/layer/pallas_call | solution.py:423
  106.6 7.3 %all-to-all-done.3.rows = bf16[128,48,128]{2,1,0:T(8,128)(2,1)} async-done(((bf16[128,48,128]{2,1,0:T(8,128)(2,1)}), bf16[128,48,128]{2,1,0:T(8,128)(2,1)}, u32[]{:S(2)}, u32[]{:S(2)}) %all-to-all-start.3) | async-done | bytes 1572896 | tf_op jit(solution)/shard_map/all_to_all | solution.py:577
  113.9 4.9 %all-to-all-start.4 = ((bf16[128,48,128]{2,1,0:T(8,128)(2,1)}), bf16[128,48,128]{2,1,0:T(8,128)(2,1)S(1)}, u32[]{:S(2)}, u32[]{:S(2)}) async-start(bf16[128,48,128]{2,1,0:T(8,128)(2,1)} %bitcast.2), calls=%async_computation.4 | async-start | bytes 3145728 | tf_op jit(solution)/shard_map/all_to_all | solution.py:577
  118.8 9.2 %collect.2 = (f32[3072,128]{1,0:T(8,128)S(1)}, s32[8,768]{1,0:T(8,128)S(1)}) custom-call(s32[128,1,384]{2,1,0:T(1,128)S(1)} %all_to_all.25.got_hbm.refs_1_.given, bf16[128,48,128]{2,1,0:T(8,128)(2,1)} %all-to-all-done.3.rows), custom_call_target="tpu_custom_call" | custom-call | flops 12000000000 | bytes 20000000 | tf_op jit(solution)/shard_map/collect/pallas_call | solution.py:539
  127.9 0.0 copy-start.3
  127.9 1.2 copy-done.3
  129.1 13.9 %all-to-all-done.4.rows = bf16[128,48,128]{2,1,0:T(8,128)(2,1)S(1)} async-done(((bf16[128,48,128]{2,1,0:T(8,128)(2,1)}), bf16[128,48,128]{2,1,0:T(8,128)(2,1)S(1)}, u32[]{:S(2)}, u32[]{:S(2)}) %all-to-all-start.4) | async-done | bytes 1572896 | tf_op jit(solution)/shard_map/all_to_all | solution.py:577
  143.0 8.0 %collect.3 = f32[3072,128]{1,0:T(8,128)} custom-call(s32[8,768]{1,0:T(8,128)S(1)} %get-tuple-element.15.given, bf16[128,48,128]{2,1,0:T(8,128)(2,1)S(1)} %all-to-all-done.4.rows, f32[3072,128]{1,0:T(8,128)} %copy-done.3), custom_call_target="tpu_custom_call" | custom-call | flops 12000000000 | bytes 20000000 | tf_op jit(solution)/shard_map/collect/pallas_call | solution.py:539
Async XLA Ops:
  57.1 3.9 %copy-start.2 = (s32[8]{0:T(128)S(1)}, s32[8]{0:T(128)}, u32[]{:S(2)}) copy-start(s32[8]{0:T(128)} %refs_0_.3) | copy-start | bytes 100
  57.1 24.4 %all-to-all-start.1 = ((bf16[16,48,1024]{2,1,0:T(8,128)(2,1)}), bf16[16,48,1024]{2,1,0:T(8,128)(2,1)S(1)}, u32[]{:S(2)}, u32[]{:S(2)}) async-start(bf16[16,48,1024]{2,1,0:T(8,128)(2,1)} %get-tuple-element.10), calls=%async_computation.1 | async-start | bytes 3145728 | tf_op jit(solution)/shard_map/all_to_all | solution.py:572
  60.9 1.2 copy-start
  81.4 8.5 %copy-start.1 = (bf16[8,64,1024]{2,1,0:T(8,128)(2,1)S(1)}, bf16[8,64,1024]{2,1,0:T(8,128)(2,1)}, u32[]{:S(2)}) copy-start(bf16[8,64,1024]{2,1,0:T(8,128)(2,1)} %refs_3_.3) | copy-start | bytes 3145732
  81.4 32.4 %all-to-all-start.3 = ((bf16[128,48,128]{2,1,0:T(8,128)(2,1)}), bf16[128,48,128]{2,1,0:T(8,128)(2,1)}, u32[]{:S(2)}, u32[]{:S(2)}) async-start(bf16[128,48,128]{2,1,0:T(8,128)(2,1)} %bitcast.1), calls=%async_computation.3 | async-start | bytes 3145728 | tf_op jit(solution)/shard_map/all_to_all | solution.py:577
  113.9 29.1 %all-to-all-start.4 = ((bf16[128,48,128]{2,1,0:T(8,128)(2,1)}), bf16[128,48,128]{2,1,0:T(8,128)(2,1)S(1)}, u32[]{:S(2)}, u32[]{:S(2)}) async-start(bf16[128,48,128]{2,1,0:T(8,128)(2,1)} %bitcast.2), calls=%async_computation.4 | async-start | bytes 3145728 | tf_op jit(solution)/shard_map/all_to_all | solution.py:577
  127.9 1.2 copy-start.3

commit v2 on v1

--- a/solution.py
+++ b/solution.py
@@ -490,7 +490,6 @@
         get_codes.start()
         get_prev.start()
         get_codes.wait()
-        get_prev.wait()
     else:
         get_ids = pltpu.make_async_copy(given.at[:, :, pl.ds(0, 128)], got, sems.at[0])
         get_ids.start()
@@ -512,6 +511,8 @@
                 here, block, jnp.zeros_like(block)
             )
     acc = dot(hits[...], wide[...])
+    if chunk:
+        get_prev.wait()
     puts = []
     for p in range(parts):
         at = slice(p * height, (p + 1) * height)

time: 152 us -> 151 us (level)
  no operation moved by 1% of the time
where the time goes in v2:
time: 151 us; the launch traced here: 150 us
  Pallas kernels  59.1 us (39%)
  blocking collectives  46.5 us (31%)
  waiting for transfers between devices  23.9 us (16%)
  starting transfers between devices  17.2 us (11%)
  local copies, waits for them, and re-layouts  2.38 us (2%)
    pallas_call x2, Pallas kernels, layer(): pl.pallas_call(functools.partial(layer_kernel, chunk), out_shape=[jax.Sha...  33.2 us
    all_to_all x1, blocking collectives, body(): fetched = lax.all_to_all(served[c], 'table', 0, 0, tiled=True)  24.4 us
    all_to_all x1, blocking collectives, body(): got = lax.all_to_all(leaving, both, 0, 0, tiled=True)  22.1 us
    all_to_all x2, waiting for transfers between devices, body(): returned.append(lax.all_to_all(grads, both, 0, 0, tiled=True))  21.2 us
    pallas_call x2, Pallas kernels, collect(): pl.pallas_call(functools.partial(collect_kernel, chunk), out_shape=result...  16 us
    all_to_all x2, starting transfers between devices, body(): returned.append(lax.all_to_all(grads, both, 0, 0, tiled=True))  13.4 us
    pallas_call x1, Pallas kernels, serve_rows(): pl.pallas_call(serve_kernel, out_shape=[jax.ShapeDtypeStruct(shape, BF)]...  7.9 us
    all_to_all x1, starting transfers between devices, body(): fetched = lax.all_to_all(served[c], 'table', 0, 0, tiled=True)  3.84 us
  transfers between devices with their start and end apart: 3, of which 3 were waited for; matrix products, arithmetic and copies ran while one was open for 0% of the time, Pallas kernels for 28%

profile of v2, /device:TPU:1, one launch (start us, length us, event | category | flops | bytes accessed | tf_op | source)
XLA Modules:
  0.0 150.0 jit_solution(6095966866146789293)
XLA Ops:
  0.6 2.0 %leaving_ids.1 = s32[128,1,384]{2,1,0:T(1,128)} custom-call(s32[8]{0:T(128)} %order_hbm.1, s32[3,8,64]{2,1,0:T(8,128)} %bitcast.4), custom_call_target="tpu_custom_call" | custom-call | tf_op jit(solution)/shard_map/leaving_ids/pallas_call | solution.py:91
  2.7 22.1 %all_to_all.25.got_hbm.refs_1_.given = s32[128,1,384]{2,1,0:T(1,128)S(1)} all-to-all(s32[128,1,384]{2,1,0:T(1,128)} %leaving_ids.1), channel_id=1, replica_groups=mesh['batch'=8,'table'=16] {'batch','table'}, dimensions={0} | all-to-all | bytes 393216 | tf_op jit(solution)/shard_map/all_to_all | solution.py:569
  24.8 7.9 %serve_rows.1 = (bf16[16,48,1024]{2,1,0:T(8,128)(2,1)S(1)}, bf16[16,48,1024]{2,1,0:T(8,128)(2,1)}) custom-call(s32[128,1,384]{2,1,0:T(1,128)S(1)} %all_to_all.25.got_hbm.refs_1_.given, bf16[3,1024,1024]{2,1,0:T(8,128)(2,1)} %table_hbm.1), custom_call_target="tpu_custom_call" | custom-call | tf_op jit(solution)/shard_map/serve_rows/pallas_call | solution.py:187
  32.7 24.4 %all_to_all.26.refs_2_ = bf16[16,48,1024]{2,1,0:T(8,128)(2,1)S(1)} all-to-all(bf16[16,48,1024]{2,1,0:T(8,128)(2,1)S(1)} %get-tuple-element.11), channel_id=1, replica_groups=mesh['batch'=8,'table'=16] {'table'}, dimensions={0} | all-to-all | bytes 3145728 | tf_op jit(solution)/shard_map/all_to_all | solution.py:573
  57.1 0.0 copy-start.2
  57.1 3.8 %all-to-all-start.1 = ((bf16[16,48,1024]{2,1,0:T(8,128)(2,1)}), bf16[16,48,1024]{2,1,0:T(8,128)(2,1)S(1)}, u32[]{:S(2)}, u32[]{:S(2)}) async-start(bf16[16,48,1024]{2,1,0:T(8,128)(2,1)} %get-tuple-element.10), calls=%async_computation.1 | async-start | bytes 3145728 | tf_op jit(solution)/shard_map/all_to_all | solution.py:573
  60.9 0.0 copy-done.2
  60.9 0.0 copy-start
  60.9 1.2 copy-done
  62.1 16.6 %layer.2 = (bf16[8,64,1024]{2,1,0:T(8,128)(2,1)}, bf16[8,16,48,128]{3,2,1,0:T(8,128)(2,1)}) custom-call(s32[8]{0:T(128)S(1)} %copy-done.2, s32[128,1,384]{2,1,0:T(1,128)S(1)} %all_to_all.25.got_hbm.refs_1_.given, bf16[16,48,1024]{2,1,0:T(8,128)(2,1)S(1)} %all_to_all.26.refs_2_, bf16[8,64,1024]{2,1,0:T(8,128)(2,1)S(1)} %copy-done, ...), custom_call_target="tpu_custom_call" | custom-call | flops 12000000000 | bytes 20000000 | tf_op jit(solution)/shard_map/layer/pallas_call | solution.py:423
  78.7 2.7 %all-to-all-done.1.refs_2_ = bf16[16,48,1024]{2,1,0:T(8,128)(2,1)S(1)} async-done(((bf16[16,48,1024]{2,1,0:T(8,128)(2,1)}), bf16[16,48,1024]{2,1,0:T(8,128)(2,1)S(1)}, u32[]{:S(2)}, u32[]{:S(2)}) %all-to-all-start.1) | async-done | bytes 1572896 | tf_op jit(solution)/shard_map/all_to_all | solution.py:573
  81.4 0.0 copy-start.1
  81.4 8.5 %all-to-all-start.3 = ((bf16[128,48,128]{2,1,0:T(8,128)(2,1)}), bf16[128,48,128]{2,1,0:T(8,128)(2,1)}, u32[]{:S(2)}, u32[]{:S(2)}) async-start(bf16[128,48,128]{2,1,0:T(8,128)(2,1)} %bitcast.1), calls=%async_computation.3 | async-start | bytes 3145728 | tf_op jit(solution)/shard_map/all_to_all | solution.py:578
  90.0 0.0 copy-done.1
  90.0 16.6 %layer.3 = (bf16[8,64,1024]{2,1,0:T(8,128)(2,1)}, bf16[8,16,48,128]{3,2,1,0:T(8,128)(2,1)}) custom-call(s32[8]{0:T(128)S(1)} %copy-done.2, s32[128,1,384]{2,1,0:T(1,128)S(1)} %all_to_all.25.got_hbm.refs_1_.given, bf16[16,48,1024]{2,1,0:T(8,128)(2,1)S(1)} %all-to-all-done.1.refs_2_, ...), custom_call_target="tpu_custom_call", output_to_operand_aliasing={{0}: (6, {})} | custom-call | flops 12000000000 | bytes 20000000 | tf_op jit(solution)/shard_map/layer/pallas_call | solution.py:423
  106.6 7.3 %all-to-all-done.3.rows = bf16[128,48,128]{2,1,0:T(8,128)(2,1)} async-done(((bf16[128,48,128]{2,1,0:T(8,128)(2,1)}), bf16[128,48,128]{2,1,0:T(8,128)(2,1)}, u32[]{:S(2)}, u32[]{:S(2)}) %all-to-all-start.3) | async-done | bytes 1572896 | tf_op jit(solution)/shard_map/all_to_all | solution.py:578
  113.9 4.9 %all-to-all-start.4 = ((bf16[128,48,128]{2,1,0:T(8,128)(2,1)}), bf16[128,48,128]{2,1,0:T(8,128)(2,1)S(1)}, u32[]{:S(2)}, u32[]{:S(2)}) async-start(bf16[128,48,128]{2,1,0:T(8,128)(2,1)} %bitcast.2), calls=%async_computation.4 | async-start | bytes 3145728 | tf_op jit(solution)/shard_map/all_to_all | solution.py:578
  118.8 9.2 %collect.2 = (f32[3072,128]{1,0:T(8,128)S(1)}, s32[8,768]{1,0:T(8,128)S(1)}) custom-call(s32[128,1,384]{2,1,0:T(1,128)S(1)} %all_to_all.25.got_hbm.refs_1_.given, bf16[128,48,128]{2,1,0:T(8,128)(2,1)} %all-to-all-done.3.rows), custom_call_target="tpu_custom_call" | custom-call | flops 12000000000 | bytes 20000000 | tf_op jit(solution)/shard_map/collect/pallas_call | solution.py:540
  127.9 0.0 copy-start.3
  127.9 1.2 copy-done.3
  129.1 13.9 %all-to-all-done.4.rows = bf16[128,48,128]{2,1,0:T(8,128)(2,1)S(1)} async-done(((bf16[128,48,128]{2,1,0:T(8,128)(2,1)}), bf16[128,48,128]{2,1,0:T(8,128)(2,1)S(1)}, u32[]{:S(2)}, u32[]{:S(2)}) %all-to-all-start.4) | async-done | bytes 1572896 | tf_op jit(solution)/shard_map/all_to_all | solution.py:578
  143.0 6.9 %collect.3 = f32[3072,128]{1,0:T(8,128)} custom-call(s32[8,768]{1,0:T(8,128)S(1)} %get-tuple-element.15.given, bf16[128,48,128]{2,1,0:T(8,128)(2,1)S(1)} %all-to-all-done.4.rows, f32[3072,128]{1,0:T(8,128)} %copy-done.3), custom_call_target="tpu_custom_call" | custom-call | flops 12000000000 | bytes 20000000 | tf_op jit(solution)/shard_map/collect/pallas_call | solution.py:540
Async XLA Ops:
  57.1 3.9 %copy-start.2 = (s32[8]{0:T(128)S(1)}, s32[8]{0:T(128)}, u32[]{:S(2)}) copy-start(s32[8]{0:T(128)} %refs_0_.3) | copy-start | bytes 100
  57.1 24.4 %all-to-all-start.1 = ((bf16[16,48,1024]{2,1,0:T(8,128)(2,1)}), bf16[16,48,1024]{2,1,0:T(8,128)(2,1)S(1)}, u32[]{:S(2)}, u32[]{:S(2)}) async-start(bf16[16,48,1024]{2,1,0:T(8,128)(2,1)} %get-tuple-element.10), calls=%async_computation.1 | async-start | bytes 3145728 | tf_op jit(solution)/shard_map/all_to_all | solution.py:573
  60.9 1.2 copy-start
  81.4 8.5 %copy-start.1 = (bf16[8,64,1024]{2,1,0:T(8,128)(2,1)S(1)}, bf16[8,64,1024]{2,1,0:T(8,128)(2,1)}, u32[]{:S(2)}) copy-start(bf16[8,64,1024]{2,1,0:T(8,128)(2,1)} %refs_3_.3) | copy-start | bytes 3145732
  81.4 32.4 %all-to-all-start.3 = ((bf16[128,48,128]{2,1,0:T(8,128)(2,1)}), bf16[128,48,128]{2,1,0:T(8,128)(2,1)}, u32[]{:S(2)}, u32[]{:S(2)}) async-start(bf16[128,48,128]{2,1,0:T(8,128)(2,1)} %bitcast.1), calls=%async_computation.3 | async-start | bytes 3145728 | tf_op jit(solution)/shard_map/all_to_all | solution.py:578
  113.9 29.1 %all-to-all-start.4 = ((bf16[128,48,128]{2,1,0:T(8,128)(2,1)}), bf16[128,48,128]{2,1,0:T(8,128)(2,1)S(1)}, u32[]{:S(2)}, u32[]{:S(2)}) async-start(bf16[128,48,128]{2,1,0:T(8,128)(2,1)} %bitcast.2), calls=%async_computation.4 | async-start | bytes 3145728 | tf_op jit(solution)/shard_map/all_to_all | solution.py:578
  127.9 1.2 copy-start.3

commit v3 on v2

--- a/solution.py
+++ b/solution.py
@@ -74,13 +74,15 @@
         total = total + dot(left, right, NT)
     codes = (total[:owners] * 64.0 + total[owners:]).astype(jnp.int32)
     slots = owner * 16 + rank
+    puts = []
     for b in range(users):
         part = pl.ds(b * owners, owners)
         out[part, 0, :128] = codes
         out[part, 0, 128:] = jnp.broadcast_to(slots[b : b + 1], (owners, lanes))
-    put = pltpu.make_async_copy(out, out_hbm, sems.at[2])
-    put.start()
-    put.wait()
+        puts.append(pltpu.make_async_copy(out.at[part], out_hbm.at[part], sems.at[2 + b]))
+        puts[-1].start()
+    for put in puts:
+        put.wait()
 
 
 def leaving_ids(order, ids, owners):
@@ -98,7 +100,7 @@
             pltpu.VMEM(ids.shape, jnp.int32),
             pltpu.VMEM((users, 256), jnp.int32),
             pltpu.VMEM(shape, jnp.int32),
-            pltpu.SemaphoreType.DMA((3,)),
+            pltpu.SemaphoreType.DMA((2 + users,)),
         ],
         compiler_params=pltpu.CompilerParams(vmem_limit_bytes=60 * MIB),
         name="leaving_ids",
@@ -128,7 +130,7 @@
     for i, (h, first) in enumerate(places):
         copies[i].wait()
 
-        @pl.loop(0, size // 64)
+        @pl.loop(0, size // 64, unroll=2)
         def _(g):
             for q in range(4):
                 at = pl.multiple_of(first + g * 64 + q * 16, 16)

time: 151 us -> 150 us (level)
  no operation moved by 1% of the time
where the time goes in v3:
time: 150 us
  Pallas kernels  59 us (39%)
  blocking collectives  46.5 us (31%)
  waiting for transfers between devices  23.9 us (16%)
  starting transfers between devices  17.2 us (11%)
  local copies, waits for them, and re-layouts  2.38 us (2%)
    pallas_call x2, Pallas kernels, layer(): pl.pallas_call(functools.partial(layer_kernel, chunk), out_shape=[jax.Sha...  33.1 us
    all_to_all x1, blocking collectives, body(): fetched = lax.all_to_all(served[c], 'table', 0, 0, tiled=True)  24.4 us
    all_to_all x1, blocking collectives, body(): got = lax.all_to_all(leaving, both, 0, 0, tiled=True)  22.1 us
    all_to_all x2, waiting for transfers between devices, body(): returned.append(lax.all_to_all(grads, both, 0, 0, tiled=True))  21.2 us
    pallas_call x2, Pallas kernels, collect(): pl.pallas_call(functools.partial(collect_kernel, chunk), out_shape=result...  16 us
    all_to_all x2, starting transfers between devices, body(): returned.append(lax.all_to_all(grads, both, 0, 0, tiled=True))  13.4 us
    pallas_call x1, Pallas kernels, serve_rows(): pl.pallas_call(serve_kernel, out_shape=[jax.ShapeDtypeStruct(shape, BF)]...  7.76 us
    all_to_all x1, starting transfers between devices, body(): fetched = lax.all_to_all(served[c], 'table', 0, 0, tiled=True)  3.84 us
  transfers between devices with their start and end apart: 3, of which 3 were waited for; matrix products, arithmetic and copies ran while one was open for 0% of the time, Pallas kernels for 28%

profile of v3, /device:TPU:1, one launch (start us, length us, event | category | flops | bytes accessed | tf_op | source)
XLA Modules:
  0.0 149.9 jit_solution(18200413879057481240)
XLA Ops:
  0.6 2.0 %leaving_ids.1 = s32[128,1,384]{2,1,0:T(1,128)} custom-call(s32[8]{0:T(128)} %order_hbm.1, s32[3,8,64]{2,1,0:T(8,128)} %bitcast.4), custom_call_target="tpu_custom_call" | custom-call | tf_op jit(solution)/shard_map/leaving_ids/pallas_call | solution.py:93
  2.7 22.1 %all_to_all.25.got_hbm.refs_1_.given = s32[128,1,384]{2,1,0:T(1,128)S(1)} all-to-all(s32[128,1,384]{2,1,0:T(1,128)} %leaving_ids.1), channel_id=1, replica_groups=mesh['batch'=8,'table'=16] {'batch','table'}, dimensions={0} | all-to-all | bytes 393216 | tf_op jit(solution)/shard_map/all_to_all | solution.py:571
  24.8 7.8 %serve_rows.1 = (bf16[16,48,1024]{2,1,0:T(8,128)(2,1)S(1)}, bf16[16,48,1024]{2,1,0:T(8,128)(2,1)}) custom-call(s32[128,1,384]{2,1,0:T(1,128)S(1)} %all_to_all.25.got_hbm.refs_1_.given, bf16[3,1024,1024]{2,1,0:T(8,128)(2,1)} %table_hbm.1), custom_call_target="tpu_custom_call" | custom-call | tf_op jit(solution)/shard_map/serve_rows/pallas_call | solution.py:189
  32.5 24.4 %all_to_all.26.refs_2_ = bf16[16,48,1024]{2,1,0:T(8,128)(2,1)S(1)} all-to-all(bf16[16,48,1024]{2,1,0:T(8,128)(2,1)S(1)} %get-tuple-element.11), channel_id=1, replica_groups=mesh['batch'=8,'table'=16] {'table'}, dimensions={0} | all-to-all | bytes 3145728 | tf_op jit(solution)/shard_map/all_to_all | solution.py:575
  56.9 0.0 copy-start.2
  56.9 3.8 %all-to-all-start.1 = ((bf16[16,48,1024]{2,1,0:T(8,128)(2,1)}), bf16[16,48,1024]{2,1,0:T(8,128)(2,1)S(1)}, u32[]{:S(2)}, u32[]{:S(2)}) async-start(bf16[16,48,1024]{2,1,0:T(8,128)(2,1)} %get-tuple-element.10), calls=%async_computation.1 | async-start | bytes 3145728 | tf_op jit(solution)/shard_map/all_to_all | solution.py:575
  60.8 0.0 copy-done.2
  60.8 0.0 copy-start
  60.8 1.2 copy-done
  62.0 16.6 %layer.2 = (bf16[8,64,1024]{2,1,0:T(8,128)(2,1)}, bf16[8,16,48,128]{3,2,1,0:T(8,128)(2,1)}) custom-call(s32[8]{0:T(128)S(1)} %copy-done.2, s32[128,1,384]{2,1,0:T(1,128)S(1)} %all_to_all.25.got_hbm.refs_1_.given, bf16[16,48,1024]{2,1,0:T(8,128)(2,1)S(1)} %all_to_all.26.refs_2_, bf16[8,64,1024]{2,1,0:T(8,128)(2,1)S(1)} %copy-done, ...), custom_call_target="tpu_custom_call" | custom-call | flops 12000000000 | bytes 20000000 | tf_op jit(solution)/shard_map/layer/pallas_call | solution.py:425
  78.6 2.7 %all-to-all-done.1.refs_2_ = bf16[16,48,1024]{2,1,0:T(8,128)(2,1)S(1)} async-done(((bf16[16,48,1024]{2,1,0:T(8,128)(2,1)}), bf16[16,48,1024]{2,1,0:T(8,128)(2,1)S(1)}, u32[]{:S(2)}, u32[]{:S(2)}) %all-to-all-start.1) | async-done | bytes 1572896 | tf_op jit(solution)/shard_map/all_to_all | solution.py:575
  81.3 0.0 copy-start.1
  81.3 8.5 %all-to-all-start.3 = ((bf16[128,48,128]{2,1,0:T(8,128)(2,1)}), bf16[128,48,128]{2,1,0:T(8,128)(2,1)}, u32[]{:S(2)}, u32[]{:S(2)}) async-start(bf16[128,48,128]{2,1,0:T(8,128)(2,1)} %bitcast.1), calls=%async_computation.3 | async-start | bytes 3145728 | tf_op jit(solution)/shard_map/all_to_all | solution.py:580
  89.8 0.0 copy-done.1
  89.8 16.6 %layer.3 = (bf16[8,64,1024]{2,1,0:T(8,128)(2,1)}, bf16[8,16,48,128]{3,2,1,0:T(8,128)(2,1)}) custom-call(s32[8]{0:T(128)S(1)} %copy-done.2, s32[128,1,384]{2,1,0:T(1,128)S(1)} %all_to_all.25.got_hbm.refs_1_.given, bf16[16,48,1024]{2,1,0:T(8,128)(2,1)S(1)} %all-to-all-done.1.refs_2_, ...), custom_call_target="tpu_custom_call", output_to_operand_aliasing={{0}: (6, {})} | custom-call | flops 12000000000 | bytes 20000000 | tf_op jit(solution)/shard_map/layer/pallas_call | solution.py:425
  106.4 7.3 %all-to-all-done.3.rows = bf16[128,48,128]{2,1,0:T(8,128)(2,1)} async-done(((bf16[128,48,128]{2,1,0:T(8,128)(2,1)}), bf16[128,48,128]{2,1,0:T(8,128)(2,1)}, u32[]{:S(2)}, u32[]{:S(2)}) %all-to-all-start.3) | async-done | bytes 1572896 | tf_op jit(solution)/shard_map/all_to_all | solution.py:580
  113.7 4.9 %all-to-all-start.4 = ((bf16[128,48,128]{2,1,0:T(8,128)(2,1)}), bf16[128,48,128]{2,1,0:T(8,128)(2,1)S(1)}, u32[]{:S(2)}, u32[]{:S(2)}) async-start(bf16[128,48,128]{2,1,0:T(8,128)(2,1)} %bitcast.2), calls=%async_computation.4 | async-start | bytes 3145728 | tf_op jit(solution)/shard_map/all_to_all | solution.py:580
  118.6 9.2 %collect.2 = (f32[3072,128]{1,0:T(8,128)S(1)}, s32[8,768]{1,0:T(8,128)S(1)}) custom-call(s32[128,1,384]{2,1,0:T(1,128)S(1)} %all_to_all.25.got_hbm.refs_1_.given, bf16[128,48,128]{2,1,0:T(8,128)(2,1)} %all-to-all-done.3.rows), custom_call_target="tpu_custom_call" | custom-call | flops 12000000000 | bytes 20000000 | tf_op jit(solution)/shard_map/collect/pallas_call | solution.py:542
  127.8 0.0 copy-start.3
  127.8 1.2 copy-done.3
  129.0 13.9 %all-to-all-done.4.rows = bf16[128,48,128]{2,1,0:T(8,128)(2,1)S(1)} async-done(((bf16[128,48,128]{2,1,0:T(8,128)(2,1)}), bf16[128,48,128]{2,1,0:T(8,128)(2,1)S(1)}, u32[]{:S(2)}, u32[]{:S(2)}) %all-to-all-start.4) | async-done | bytes 1572896 | tf_op jit(solution)/shard_map/all_to_all | solution.py:580
  142.8 6.9 %collect.3 = f32[3072,128]{1,0:T(8,128)} custom-call(s32[8,768]{1,0:T(8,128)S(1)} %get-tuple-element.15.given, bf16[128,48,128]{2,1,0:T(8,128)(2,1)S(1)} %all-to-all-done.4.rows, f32[3072,128]{1,0:T(8,128)} %copy-done.3), custom_call_target="tpu_custom_call" | custom-call | flops 12000000000 | bytes 20000000 | tf_op jit(solution)/shard_map/collect/pallas_call | solution.py:542
Async XLA Ops:
  56.9 3.9 %copy-start.2 = (s32[8]{0:T(128)S(1)}, s32[8]{0:T(128)}, u32[]{:S(2)}) copy-start(s32[8]{0:T(128)} %refs_0_.3) | copy-start | bytes 100
  56.9 24.4 %all-to-all-start.1 = ((bf16[16,48,1024]{2,1,0:T(8,128)(2,1)}), bf16[16,48,1024]{2,1,0:T(8,128)(2,1)S(1)}, u32[]{:S(2)}, u32[]{:S(2)}) async-start(bf16[16,48,1024]{2,1,0:T(8,128)(2,1)} %get-tuple-element.10), calls=%async_computation.1 | async-start | bytes 3145728 | tf_op jit(solution)/shard_map/all_to_all | solution.py:575
  60.8 1.2 copy-start
  81.3 8.5 %copy-start.1 = (bf16[8,64,1024]{2,1,0:T(8,128)(2,1)S(1)}, bf16[8,64,1024]{2,1,0:T(8,128)(2,1)}, u32[]{:S(2)}) copy-start(bf16[8,64,1024]{2,1,0:T(8,128)(2,1)} %refs_3_.3) | copy-start | bytes 3145732
  81.3 32.4 %all-to-all-start.3 = ((bf16[128,48,128]{2,1,0:T(8,128)(2,1)}), bf16[128,48,128]{2,1,0:T(8,128)(2,1)}, u32[]{:S(2)}, u32[]{:S(2)}) async-start(bf16[128,48,128]{2,1,0:T(8,128)(2,1)} %bitcast.1), calls=%async_computation.3 | async-start | bytes 3145728 | tf_op jit(solution)/shard_map/all_to_all | solution.py:580
  113.7 29.1 %all-to-all-start.4 = ((bf16[128,48,128]{2,1,0:T(8,128)(2,1)}), bf16[128,48,128]{2,1,0:T(8,128)(2,1)S(1)}, u32[]{:S(2)}, u32[]{:S(2)}) async-start(bf16[128,48,128]{2,1,0:T(8,128)(2,1)} %bitcast.2), calls=%async_computation.4 | async-start | bytes 3145728 | tf_op jit(solution)/shard_map/all_to_all | solution.py:580
  127.8 1.2 copy-start.3
